TPU v7x, 32 devices: a whole 2x2x4 slice. The times are simulated.
32 devices in a mesh: grp: 2 (over x), gx: 8 (over z, y), gy: 2 (over core).
Axes of the slice: x: 2, y: 2, z: 4, core: 2. Of those that a mesh axis runs over, the one named last changes fastest.
Arguments:
- loaded_fields: bfloat16 [2, 32, 16, 128], P(None, ('grp', 'gx'), 'gy'), parts along dimension 1, may hold values from -6 to 6
- brick_home: int32 [16], P('grp'), parts along dimension 0, may hold values from 0 to 7, each once
- liquid_mask: int32 [32, 16, 128], P(('grp', 'gx'), 'gy'), parts along dimension 0, may hold values 0 or 1
- density_class: int32 [32, 16, 128], P(('grp', 'gx'), 'gy'), parts along dimension 0, may hold values from 0 to 3
- inverse_density: float32 [4], replicated, may hold values from 0.25 to 4
- conv_a: bfloat16 [27, 64, 3], replicated, may hold values from -0.625 to 0.625
- bias_a: float32 [64], replicated, may hold values from -3 to 3
- conv_b: bfloat16 [27, 64, 64], replicated, may hold values from -0.15625 to 0.15625
- bias_b: float32 [64], replicated, may hold values from -3 to 3
- conv_c: bfloat16 [27, 64, 64], replicated, may hold values from -0.15625 to 0.15625
- bias_c: float32 [64], replicated, may hold values from -3 to 3
- head_weight: bfloat16 [64], replicated, may hold values from -0.75 to 0.75
- head_bias: float32 [1], replicated, may hold values from -3 to 3
Outputs:
- pressure: float32 [32, 16, 128], P(('grp', 'gx'), 'gy'), parts along dimension 0
- loss: float32 [2], P('grp'), parts along dimension 0
- grad_conv_a: float32 [54, 64, 3], P('grp'), parts along dimension 0
- grad_bias_a: float32 [128], P('grp'), parts along dimension 0
- grad_conv_b: float32 [54, 64, 64], P('grp'), parts along dimension 0
- grad_bias_b: float32 [128], P('grp'), parts along dimension 0
- grad_conv_c: float32 [54, 64, 64], P('grp'), parts along dimension 0
- grad_bias_c: float32 [128], P('grp'), parts along dimension 0
- grad_head_weight: float32 [128], P('grp'), parts along dimension 0
There are 2 independent parts, one for each index of `grp`. A program takes and returns all parts, laid end to end along the dimension named above; an argument that names none is the same for every part. Nothing has to cross between parts.
Inputs may be any that keep to these rules, and one draw needn't show every extreme that they name: `brick_home`: a permutation of 0 to 7.
All inputs are finite; a program needn't handle non-finite values. No bound on the sum of `liquid_mask` on one device may be relied on, other than what follows from the above.
Results may differ from a plain program's by a relative error of at most 0.0041.
The roundings to bfloat16 on the way count: a program that leaves them out, or rounds other values in their place, can miss the bound.
Values may be sent and summed in bfloat16 or wider, within the bound.
A program may use at most 64 MiB of HBM per device.

v0:
```python
import functools

import jax
import jax.numpy as jnp
from jax import lax
from jax.experimental import pallas as pl
from jax.experimental.pallas import tpu as pltpu
from jax.sharding import PartitionSpec as P

F32 = jnp.float32
BF16 = jnp.bfloat16
MESH = pl.DeviceIdType.MESH
ZL = 128


def roll_up(v):
    z = lax.broadcasted_iota(jnp.int32, v.shape, 1) % ZL
    return jnp.where(z == 0, 0.0, pltpu.roll(v, 1, 1))


def roll_down(v):
    z = lax.broadcasted_iota(jnp.int32, v.shape, 1) % ZL
    return jnp.where(z == ZL - 1, 0.0, pltpu.roll(v, v.shape[1] - 1, 1))


def sigmoid(v):
    return 1.0 / (1.0 + jnp.exp(-v))


def slope(v):
    s = sigmoid(v)
    return s * (1.0 + v * (1.0 - s))


def kernel(
    n, cells,
    home, invd, hbias,
    payload, wa, wb, wc, tb, tc, ba, bb, bc, hw,
    pressure, gwa, gwb, gwc, small,
    gath, fwin, x0, h1, z1, h2, z2, z3, h3, im, im2, pv, yb, coef, gsr, g3e, g2e,
    gs_sem, gr_sem, ps_sem, pr_sem, es_sem, er_sem,
):
    gx = lax.axis_index("gx")
    gy = lax.axis_index("gy")
    count = 2 * n
    me = gx * 2 + gy
    other = 1 - gy

    pv[...] = jnp.zeros_like(pv)
    for ext in (g3e, g2e):
        ext[0] = jnp.zeros((64, 1280), BF16)
        ext[3] = jnp.zeros((64, 1280), BF16)
        for x in (1, 2):
            ext[x, :, 0:128] = jnp.zeros((64, 128), BF16)
            ext[x, :, 1152:1280] = jnp.zeros((64, 128), BF16)

    barrier = pltpu.get_barrier_semaphore()
    for k in range(1, count):
        to = lax.rem(me + k, count)
        pl.semaphore_signal(
            barrier, inc=1, device_id={"gx": to // 2, "gy": to % 2}, device_id_type=MESH
        )
    pl.semaphore_wait(barrier, count - 1)

    def gather_copy(k):
        to = lax.rem(me + k, count)
        return pltpu.make_async_remote_copy(
            src_ref=payload,
            dst_ref=gath.at[me],
            send_sem=gs_sem.at[k],
            recv_sem=gr_sem.at[k],
            device_id={"gx": to // 2, "gy": to % 2},
            device_id_type=MESH,
        )

    for k in range(1, count):
        gather_copy(k).start()
    gath[me] = payload[...]
    fwin[...] = jnp.zeros_like(fwin)
    x0[...] = jnp.zeros_like(x0)
    for k in range(1, count):
        gather_copy(k).wait_recv()
    for k in range(1, count):
        gather_copy(k).wait_send()

    for d in range(-2, 3):
        q = gx + d
        valid = jnp.logical_and(q >= 0, q < n)
        geo = jnp.clip(q, 0, n - 1)
        source = jnp.int32(0)
        for s in range(n):
            source = jnp.where(home[s] == q, s, source)
        keep = jnp.where(valid, 1.0, 0.0)
        for w in range(2):
            fields = gath[source * 2 + w].astype(F32)[0:32] * keep
            shape = gath[geo * 2 + w].astype(F32)[32:64] * keep
            both = [fields[0:16], fields[16:32], shape[0:16], shape[16:32]]
            for x in range(2):
                p = 2 * d + x + 3
                if p < 0 or p > 7:
                    continue
                for c in range(4):
                    fwin[c, p, 8 + 8 * w : 16 + 8 * w, :] = both[c][8 * x : 8 * x + 8]

    def spread(p, carry):
        for c in range(3):
            for y in range(14):
                x0[p, c : c + 1, y * 128 : (y + 1) * 128] = fwin[c, p, pl.ds(8 * gy + 5 + y, 1), :]
        return carry

    lax.fori_loop(0, 8, spread, 0)

    def merge_forward(out):
        return roll_up(out[0:64]) + out[64:128] + roll_down(out[128:192])

    def merge_back(out):
        return roll_down(out[0:64]) + out[64:128] + roll_up(out[128:192])

    def patches_a(first, lane, width):
        rows = []
        for a in range(3):
            for b in range(3):
                rows.append(x0[first + a, :, lane + b * 128 : lane + b * 128 + width])
        return jnp.concatenate(rows, axis=0).astype(BF16)

    def fill(dst, src, first, lane, width):
        for a in range(3):
            for b in range(3):
                k = (3 * a + b) * 64
                dst[k : k + 64, 0:width] = src[first + a, :, lane + b * 128 : lane + b * 128 + width]

    def layer_a(x, carry):
        out = jnp.dot(wa[...], patches_a(x, 0, 1536), preferred_element_type=F32)
        z = merge_forward(out) + ba[...]
        z1[x] = z
        h1[x] = (z * sigmoid(z) * x0[x + 1, 2:3, 128 : 128 + 1536]).astype(BF16)
        return carry

    lax.fori_loop(0, 6, layer_a, 0)

    def layer_b(x, carry):
        fill(im, h1, x, 0, 1280)
        out = jnp.dot(wb[...], im[...], preferred_element_type=F32)
        z = merge_forward(out) + bb[...]
        z2[x] = z
        h2[x] = (z * sigmoid(z) * x0[x + 2, 2:3, 256 : 256 + 1280]).astype(BF16)
        return carry

    lax.fori_loop(0, 4, layer_b, 0)

    def layer_c(x, carry):
        fill(im2.at[x], h2, x, 0, 1024)
        out = jnp.dot(wc[...], im2[x], preferred_element_type=F32)
        z = merge_forward(out) + bc[...]
        z3[x] = z
        liquid = x0[x + 3, 2:3, 384 : 384 + 1024]
        h = (z * sigmoid(z) * liquid).astype(BF16).astype(F32)
        h3[x] = h
        score = liquid * (jnp.sum(h * hw[...], axis=0, keepdims=True) + hbias[0])
        for y in range(8):
            pv[0, 1 + x, 8 + y : 9 + y, :] = score[:, y * 128 : (y + 1) * 128]
        return carry

    lax.fori_loop(0, 2, layer_c, 0)
    for x in range(2):
        pressure[x] = pv[0, 1 + x, 8:16, :]

    has_low = gx > 0
    has_high = gx < n - 1
    low = jnp.maximum(gx - 1, 0)
    high = jnp.minimum(gx + 1, n - 1)

    def face_copies(k):
        def make(slot, src, dst, to_x, to_y):
            return pltpu.make_async_remote_copy(
                src_ref=src,
                dst_ref=dst,
                send_sem=ps_sem.at[k, slot],
                recv_sem=pr_sem.at[k, slot],
                device_id={"gx": to_x, "gy": to_y},
                device_id_type=MESH,
            )

        inner = pl.ds(8, 8)
        down = make(0, pv.at[k, 1, inner], pv.at[k, 3, inner], low, gy)
        up = make(1, pv.at[k, 2, inner], pv.at[k, 0, inner], high, gy)
        side = make(2, pv.at[k, pl.ds(1, 2), inner], yb.at[k], gx, other)
        return down, up, side

    def edge_copies(k, ext):
        def make(slot, src, dst, to_x, to_y):
            return pltpu.make_async_remote_copy(
                src_ref=src,
                dst_ref=dst,
                send_sem=es_sem.at[k, slot],
                recv_sem=er_sem.at[k, slot],
                device_id={"gx": to_x, "gy": to_y},
                device_id_type=MESH,
            )

        inner = pl.ds(128, 1024)
        mine = pl.ds(pl.multiple_of(128 * (8 - 7 * gy), 128), 128)
        theirs = pl.ds(pl.multiple_of(1152 * gy, 128), 128)
        down = make(0, ext.at[1, :, inner], ext.at[3, :, inner], low, gy)
        up = make(1, ext.at[2, :, inner], ext.at[0, :, inner], high, gy)
        side = make(2, ext.at[pl.ds(1, 2), :, mine], ext.at[pl.ds(1, 2), :, theirs], gx, other)
        corner_down = make(3, ext.at[1, :, mine], ext.at[3, :, theirs], low, other)
        corner_up = make(4, ext.at[2, :, mine], ext.at[0, :, theirs], high, other)
        return down, up, side, corner_down, corner_up

    def start_all(copies):
        @pl.when(has_low)
        def _():
            for c in copies[0::3]:
                c.start()

        @pl.when(has_high)
        def _():
            for c in copies[1::3]:
                c.start()

        copies[2].start()

    def finish_all(copies):
        @pl.when(has_high)
        def _():
            for c in copies[0::3]:
                c.wait_recv()

        @pl.when(has_low)
        def _():
            for c in copies[1::3]:
                c.wait_recv()

        copies[2].wait_recv()

        @pl.when(has_low)
        def _():
            for c in copies[0::3]:
                c.wait_send()

        @pl.when(has_high)
        def _():
            for c in copies[1::3]:
                c.wait_send()

        copies[2].wait_send()

    start_all(face_copies(0))

    def geometry(p):
        window = pl.ds(pl.multiple_of(8 * gy, 8), 24)
        liquid = fwin[2, p, window, :]
        kind = fwin[3, p, window, :]
        scale = jnp.zeros_like(kind)
        for c in range(4):
            scale = scale + jnp.where(kind == c, invd[c], 0.0)
        return scale * liquid, liquid

    geo = [geometry(p) for p in range(2, 6)]
    for x in range(2):
        scaled, liquid = geo[x + 1]
        s0, l0 = scaled[8:16], liquid[8:16]
        nears = [
            tuple(v[8:16] for v in geo[x + 2]),
            tuple(v[8:16] for v in geo[x]),
            (scaled[9:17], liquid[9:17]),
            (scaled[7:15], liquid[7:15]),
            (roll_down(s0), roll_down(l0)),
            (roll_up(s0), roll_up(l0)),
        ]
        for j, (ns, nl) in enumerate(nears):
            coef[x, j] = 0.5 * (s0 * nl + ns * l0)

    def operate(k, x):
        v = pv[k, 1 + x, 8:16, :]
        nears = [
            pv[k, 2 + x, 8:16, :],
            pv[k, x, 8:16, :],
            pv[k, 1 + x, 9:17, :],
            pv[k, 1 + x, 7:15, :],
            pltpu.roll(v, ZL - 1, 1),
            pltpu.roll(v, 1, 1),
        ]
        total = jnp.zeros_like(v)
        for j, near in enumerate(nears):
            total = total + coef[x, j] * (near - v)
        return total

    def sides(k):
        for x in range(2):
            pv[k, 1 + x, 7:8, :] = yb[k, x, 7:8, :]
            pv[k, 1 + x, 16:17, :] = yb[k, x, 0:1, :]

    here = pl.ds(pl.multiple_of(8 * gy + 8, 8), 8)
    finish_all(face_copies(0))
    sides(0)
    squares = jnp.zeros((8, 128), F32)
    for x in range(2):
        residual = operate(0, x) - fwin[2, 3 + x, here, :] * fwin[1, 3 + x, here, :]
        squares = squares + residual * residual
        pv[1, 1 + x, 8:16, :] = 2.0 * residual / cells
    start_all(face_copies(1))
    loss = jnp.sum(jnp.sum(squares, axis=1, keepdims=True), axis=0, keepdims=True) / cells
    finish_all(face_copies(1))
    sides(1)
    for x in range(2):
        score = fwin[2, 3 + x, here, :] * operate(1, x)
        for y in range(8):
            gsr[x, :, y * 128 : (y + 1) * 128] = score[y : y + 1, :]

    def sum_cells(v):
        return jnp.sum(v, axis=1, keepdims=True)

    def three(g):
        gf = g.astype(F32)
        return jnp.concatenate([roll_down(gf), gf, roll_up(gf)], axis=0).astype(BF16)

    def wgrad(g, rows):
        return lax.dot_general(
            three(g), rows, (((1,), (1,)), ((), ())), preferred_element_type=F32
        )

    inner = slice(128, 1152)
    grad_head = jnp.zeros((64, 1), F32)
    grad_bc = jnp.zeros((64, 1), F32)
    for x in range(2):
        gs = gsr[x]
        liquid = x0[x + 3, 2:3, 384 : 384 + 1024]
        g = (gs * hw[...] * liquid * slope(z3[x])).astype(BF16)
        g3e[1 + x, :, inner] = g
    start_all(edge_copies(0, g3e))
    for x in range(2):
        grad_head = grad_head + sum_cells(gsr[x] * h3[x])
        g = g3e[1 + x, :, inner]
        grad_bc = grad_bc + sum_cells(g.astype(F32))
        part = wgrad(g, im2[x])
        gwc[...] = part if x == 0 else gwc[...] + part
    finish_all(edge_copies(0, g3e))

    def fill_back(dst, src, x):
        for a in range(3):
            for b in range(3):
                k = (3 * a + b) * 64
                dst[k : k + 64, :] = src[x + 2 - a, :, (2 - b) * 128 : (2 - b) * 128 + 1024]

    grad_bb = jnp.zeros((64, 1), F32)
    for x in range(2):
        fill_back(im2.at[x], g3e, x)
        out = jnp.dot(tc[...], im2[x], preferred_element_type=F32)
        liquid = x0[x + 3, 2:3, 384 : 384 + 1024]
        g = merge_back(out) * liquid * slope(z2[x + 1, :, 128 : 128 + 1024])
        g2e[1 + x, :, inner] = g.astype(BF16)
    start_all(edge_copies(1, g2e))
    for x in range(2):
        fill(im2.at[x], h1, x + 1, 128, 1024)
        g = g2e[1 + x, :, inner]
        grad_bb = grad_bb + sum_cells(g.astype(F32))
        part = wgrad(g, im2[x])
        gwb[...] = part if x == 0 else gwb[...] + part
    finish_all(edge_copies(1, g2e))

    grad_ba = jnp.zeros((64, 1), F32)
    for x in range(2):
        fill_back(im2.at[x], g2e, x)
        out = jnp.dot(tb[...], im2[x], preferred_element_type=F32)
        liquid = x0[x + 3, 2:3, 384 : 384 + 1024]
        g = (merge_back(out) * liquid * slope(z1[x + 2, :, 256 : 256 + 1024])).astype(BF16)
        grad_ba = grad_ba + sum_cells(g.astype(F32))
        part = wgrad(g, patches_a(x + 2, 256, 1024))
        gwa[...] = part if x == 0 else gwa[...] + part

    lane = lax.broadcasted_iota(jnp.int32, (64, 128), 1)
    packed = jnp.where(lane == 0, grad_ba, 0.0)
    packed = jnp.where(lane == 1, grad_bb, packed)
    packed = jnp.where(lane == 2, grad_bc, packed)
    packed = jnp.where(lane == 3, grad_head, packed)
    packed = jnp.where(lane == 4, loss, packed)
    small[...] = packed


def on_device(
    loaded_fields, brick_home, liquid_mask, density_class, inverse_density,
    conv_a, bias_a, conv_b, bias_b, conv_c, bias_c, head_weight, head_bias,
):
    n = lax.axis_size("gx")
    count = 2 * n
    payload = jnp.concatenate(
        [
            loaded_fields.reshape(32, 128),
            liquid_mask.astype(BF16).reshape(16, 128),
            density_class.astype(BF16).reshape(16, 128),
        ],
        axis=0,
    )

    def forward(w):
        w = w.reshape(3, 3, 3, 64, w.shape[-1]).transpose(2, 3, 0, 1, 4)
        return w.reshape(192, -1)

    def backward(w):
        return w.reshape(3, 3, 3, 64, 64).transpose(2, 4, 0, 1, 3).reshape(192, 576)

    wa = forward(jnp.pad(conv_a, ((0, 0), (0, 0), (0, 5))))
    vmem = pl.BlockSpec(memory_space=pltpu.VMEM)
    smem = pl.BlockSpec(memory_space=pltpu.SMEM)
    pressure, gwa, gwb, gwc, small = pl.pallas_call(
        functools.partial(kernel, n, float(2 * n * 16 * 128)),
        out_shape=(
            jax.ShapeDtypeStruct((2, 8, 128), F32),
            jax.ShapeDtypeStruct((192, 72), F32),
            jax.ShapeDtypeStruct((192, 576), F32),
            jax.ShapeDtypeStruct((192, 576), F32),
            jax.ShapeDtypeStruct((64, 128), F32),
        ),
        in_specs=[smem] * 3 + [vmem] * 10,
        out_specs=(vmem,) * 5,
        scratch_shapes=[
            pltpu.VMEM((count, 64, 128), BF16),
            pltpu.VMEM((4, 8, 32, 128), F32),
            pltpu.VMEM((8, 8, 14 * 128), F32),
            pltpu.VMEM((6, 64, 1536), BF16),
            pltpu.VMEM((6, 64, 1536), F32),
            pltpu.VMEM((4, 64, 1280), BF16),
            pltpu.VMEM((4, 64, 1280), F32),
            pltpu.VMEM((2, 64, 1024), F32),
            pltpu.VMEM((2, 64, 1024), F32),
            pltpu.VMEM((576, 1280), BF16),
            pltpu.VMEM((2, 576, 1024), BF16),
            pltpu.VMEM((2, 4, 24, 128), F32),
            pltpu.VMEM((2, 2, 8, 128), F32),
            pltpu.VMEM((2, 6, 8, 128), F32),
            pltpu.VMEM((2, 1, 1024), F32),
            pltpu.VMEM((4, 64, 1280), BF16),
            pltpu.VMEM((4, 64, 1280), BF16),
            pltpu.SemaphoreType.DMA((count,)),
            pltpu.SemaphoreType.DMA((count,)),
            pltpu.SemaphoreType.DMA((2, 3)),
            pltpu.SemaphoreType.DMA((2, 3)),
            pltpu.SemaphoreType.DMA((2, 5)),
            pltpu.SemaphoreType.DMA((2, 5)),
        ],
        compiler_params=pltpu.CompilerParams(
            collective_id=0, has_side_effects=True, vmem_limit_bytes=48 * 1024 * 1024
        ),
    )(
        brick_home, inverse_density, head_bias,
        payload, wa, forward(conv_b), forward(conv_c), backward(conv_b), backward(conv_c),
        bias_a.reshape(64, 1), bias_b.reshape(64, 1), bias_c.reshape(64, 1),
        head_weight.astype(F32).reshape(64, 1),
    )
    gwa, gwb, gwc, small = lax.psum((gwa, gwb, gwc, small), ("gx", "gy"))

    def taps(g, width):
        g = g.reshape(3, 64, 3, 3, -1)[..., :width].transpose(2, 3, 0, 1, 4)
        return g.reshape(27, 64, width)

    return (
        pressure, small[0, 4:5],
        taps(gwa, 3), small[:, 0], taps(gwb, 64), small[:, 1], taps(gwc, 64), small[:, 2],
        small[:, 3],
    )


def solution(mesh):
    placed = (
        P(None, ("grp", "gx"), "gy", None),
        P("grp"),
        P(("grp", "gx"), "gy", None),
        P(("grp", "gx"), "gy", None),
    ) + (P(),) * 9
    return jax.shard_map(
        on_device,
        mesh=mesh,
        in_specs=placed,
        out_specs=(
            P(("grp", "gx"), "gy", None),
            P("grp"),
            P("grp", None, None),
            P("grp"),
            P("grp", None, None),
            P("grp"),
            P("grp", None, None),
            P("grp"),
            P("grp"),
        ),
        check_vma=False,
    )
```

profile of v0, /device:TPU:0, one launch (start us, length us, event | category | flops | bytes accessed | tf_op | source)
XLA Modules:
  0.0 259.9 jit_solution(2622889545337209714)
XLA Ops:
  7.2 1.7 copy.50
  9.0 0.4 copy.64
  9.4 0.8 copy.51
  10.3 0.4 copy.63
  11.4 0.1 reshape.89
  12.0 0.4 reshape.94.tb
  12.5 0.4 reshape.91.wb
  12.9 0.4 reshape.95.tc
  13.3 0.4 reshape.93.wc
  13.8 41.0 %shard_map.196 = (f32[2,8,128]{2,1,0:T(8,128)S(1)}, f32[192,72]{1,0:T(8,128)S(1)}, f32[192,576]{1,0:T(8,128)S(1)}, f32[192,576]{1,0:T(8,128)S(1)}, f32[64,128]{1,0:T(8,128)}) custom-call(s32[8]{0:T(128)S(1)} %copy-done, f32[4]{0:T(128)S(1)} %copy-done.1, f32[1]{0:T(128)S(6)} %copy.70.hbias, bf16[64,128]{1,0:T(8,128)(2,1)S(1)} %pad_maximum_fusion.payload, ...), custom_call_target="tpu_custom_call" | custom-call | tf_op jit(solution)/shard_map/pallas_call | solution.py:407
  54.9 0.8 reshape.101
  55.7 0.5 reshape.103
  56.2 1.0 copy.59
  57.3 0.5 reshape.105
  57.8 1.0 copy.60
  58.8 89.3 %all-reduce.6.cloned.1.call-done = (f32[64,128]{1,0:T(8,128)}, f32[3,64,3,3,8]{1,0,4,3,2:T(4,128)}) async-done(((f32[64,128]{1,0:T(8,128)}, f32[3,64,3,3,8]{1,0,4,3,2:T(4,128)}), (f32[64,128]{1,0:T(8,128)}, f32[3,64,3,3,8]{1,0,4,3,2:T(4,128)})) %all-reduce.6.cloned.1.call-update) | async-done | bytes 88080 | tf_op jit(solution)/shard_map/psum | solution.py:452
  148.2 1.2 slice.24
  149.4 0.8 slice_bitcast_fusion
  150.3 0.6 reshape.102
  150.9 1.7 slice_reduce_fusion
  152.6 96.8 %all-reduce.8.cloned.1.call-done = (f32[27,64,64]{2,1,0:T(8,128)}, f32[27,64,64]{2,1,0:T(8,128)}) async-done(((f32[27,64,64]{2,1,0:T(8,128)}, f32[27,64,64]{2,1,0:T(8,128)}), (f32[27,64,64]{2,1,0:T(8,128)}, f32[27,64,64]{2,1,0:T(8,128)})) %all-reduce.8.cloned.1.call-update) | async-done | bytes 884752 | tf_op jit(solution)/shard_map/psum | solution.py:452
  249.4 0.6 copy.71
  250.0 2.2 copy.72
  252.2 0.9 copy.73
  (43 shorter events, 0.9 us)
Async XLA Ops:
  7.2 1.8 copy-start.2
  7.2 2.2 copy-start.3
  7.2 141.0 %all-reduce.6.cloned.1.call-start = ((), (), s32[]{:S(2)}) async-start(), calls=%async_computation | async-start | bytes 360448 | tf_op jit(solution)/shard_map/psum | solution.py:452
  9.4 1.9 copy-start.12
  9.4 1.9 copy-start.5
  9.4 2.3 copy-start.9
  9.4 2.4 copy-start.10
  9.4 2.5 copy-start.11
  12.4 1.3 copy-start.6
  12.5 1.3 copy-start.7
  12.5 1.3 copy-start.8
  12.5 1.3 copy-start
  12.5 1.3 copy-start.1
  55.7 193.7 %all-reduce.8.cloned.1.call-start = ((), (), s32[]{:S(2)}) async-start(), calls=%async_computation.1 | async-start | bytes 3538944 | tf_op jit(solution)/shard_map/psum | solution.py:452
  249.4 2.8 %copy-start.4 = (f32[27,64,64]{2,1,0:T(8,128)S(1)}, f32[27,64,64]{2,1,0:T(8,128)}, u32[]{:S(2)}) copy-start(f32[27,64,64]{2,1,0:T(8,128)} %get-tuple-element.44) | copy-start | bytes 1327108
Sparse Core Ops, SparseCore 0:
  55.8 92.3 all-reduce.5
  152.3 97.0 all-reduce.7
where the time goes:
time: 260 us
  waiting for transfers between devices  186 us (72%)
  Pallas kernels  41 us (16%)
  local copies, waits for them, and re-layouts  17.6 us (7%)
  between operations  15 us (6%)
    psum x2, waiting for transfers between devices, on_device(): gwa, gwb, gwc, small = lax.psum((gwa, gwb, gwc, small), ('gx', 'gy'))  186 us
    pallas_call x1, Pallas kernels, on_device(): pl.pallas_call(functools.partial(kernel, n, float(2 * n * 16 * 128)), out...  41 us
  transfers between devices with their start and end apart: 2, of which 2 were waited for; matrix products, arithmetic and copies ran while one was open for 3% of the time, Pallas kernels for 0%

commit v1 on v0

--- a/solution.py
+++ b/solution.py
@@ -33,12 +33,13 @@
 
 
 def kernel(
-    n, cells,
+    n, cells, chunks,
     home, invd, hbias,
-    payload, wa, wb, wc, tb, tc, ba, bb, bc, hw,
-    pressure, gwa, gwb, gwc, small,
+    payload, wa, cb, cc, ba, bb, bc, hw,
+    pressure, out_a, out_b, out_c, small,
     gath, fwin, x0, h1, z1, h2, z2, z3, h3, im, im2, pv, yb, coef, gsr, g3e, g2e,
-    gs_sem, gr_sem, ps_sem, pr_sem, es_sem, er_sem,
+    wb, wc, tb, tc, gwa, gwb, gwc, raw_c, raw_b, near_c, near_b, sum_c, sum_b, land_c, land_b, full_c, full_b, tiny,
+    gs_sem, gr_sem, ps_sem, pr_sem, es_sem, er_sem, ws_sem, wr_sem, ts_sem, tr_sem,
 ):
     gx = lax.axis_index("gx")
     gy = lax.axis_index("gy")
@@ -47,6 +48,8 @@
     other = 1 - gy
 
     pv[...] = jnp.zeros_like(pv)
+    raw_c[...] = jnp.zeros_like(raw_c)
+    raw_b[...] = jnp.zeros_like(raw_b)
     for ext in (g3e, g2e):
         ext[0] = jnp.zeros((64, 1280), BF16)
         ext[3] = jnp.zeros((64, 1280), BF16)
@@ -78,6 +81,10 @@
     gath[me] = payload[...]
     fwin[...] = jnp.zeros_like(fwin)
     x0[...] = jnp.zeros_like(x0)
+    for wide, conv in ((wb, cb), (wc, cc)):
+        for t in range(27):
+            k, e = t // 3 * 64, t % 3 * 64
+            wide[e : e + 64, k : k + 64] = conv[t]
     for k in range(1, count):
         gather_copy(k).wait_recv()
     for k in range(1, count):
@@ -247,6 +254,11 @@
         copies[2].wait_send()
 
     start_all(face_copies(0))
+    for x in range(2):
+        z3[x] = x0[x + 3, 2:3, 384 : 384 + 1024] * slope(z3[x])
+    for t in range(27):
+        k, e = t // 3 * 64, t % 3 * 64
+        tc[e : e + 64, k : k + 64] = cc[t].astype(F32).T.astype(BF16)
 
     def geometry(p):
         window = pl.ds(pl.multiple_of(8 * gy, 8), 24)
@@ -301,6 +313,13 @@
         squares = squares + residual * residual
         pv[1, 1 + x, 8:16, :] = 2.0 * residual / cells
     start_all(face_copies(1))
+    for x in range(2):
+        liquid = x0[x + 3, 2:3, 384 : 384 + 1024]
+        z2[x + 1, :, 128 : 128 + 1024] = liquid * slope(z2[x + 1, :, 128 : 128 + 1024])
+        z1[x + 2, :, 256 : 256 + 1024] = liquid * slope(z1[x + 2, :, 256 : 256 + 1024])
+    for t in range(27):
+        k, e = t // 3 * 64, t % 3 * 64
+        tb[e : e + 64, k : k + 64] = cb[t].astype(F32).T.astype(BF16)
     loss = jnp.sum(jnp.sum(squares, axis=1, keepdims=True), axis=0, keepdims=True) / cells
     finish_all(face_copies(1))
     sides(1)
@@ -322,12 +341,99 @@
         )
 
     inner = slice(128, 1152)
+    raws, nears, sums = (raw_c, raw_b), (near_c, near_b), (sum_c, sum_b)
+    lands, fulls = (land_c, land_b), (full_c, full_b)
+
+    def weight_copy(i, slot, src, dst, to_x, to_y):
+        return pltpu.make_async_remote_copy(
+            src_ref=src,
+            dst_ref=dst,
+            send_sem=ws_sem.at[i, slot],
+            recv_sem=wr_sem.at[i, slot],
+            device_id={"gx": to_x, "gy": to_y},
+            device_id_type=MESH,
+        )
+
+    def rows_at(start, length):
+        return pl.ds(pl.multiple_of(start, 16), length)
+
+    def pair_copy(i):
+        half = n * chunks[i]
+        return weight_copy(i, 0, raws[i].at[rows_at(other * half, half)], nears[i], gx, other)
+
+    def scatter_copies(i):
+        c = chunks[i]
+        made = []
+        for k in range(1, n):
+            to = lax.rem(gx + k, n)
+            made.append(
+                weight_copy(i, 2 + k, sums[i].at[rows_at(to * c, c)], lands[i].at[k], to, gy)
+            )
+        return made
+
+    def gather_copies(i):
+        c = chunks[i]
+        place = fulls[i].at[rows_at((gy * n + gx) * c, c)]
+        return [
+            weight_copy(i, 2 + n + k, place, place, lax.rem(gx + k, n), gy) for k in range(1, n)
+        ]
+
+    def last_copy(i):
+        half = n * chunks[i]
+        place = fulls[i].at[rows_at(gy * half, half)]
+        return weight_copy(i, 1, place, place, gx, other)
+
+    def wait_copies(copies):
+        for c in copies:
+            c.wait_recv()
+        for c in copies:
+            c.wait_send()
+
+    def start_copies(copies):
+        for c in copies:
+            c.start()
+
+    def pair_to_scatter(i):
+        half = n * chunks[i]
+        wait_copies([pair_copy(i)])
+        mine = raws[i][rows_at(gy * half, half), :].astype(F32)
+        sums[i][...] = (mine + nears[i][...].astype(F32)).astype(BF16)
+        start_copies(scatter_copies(i))
+
+    def scatter_to_gather(i):
+        c = chunks[i]
+        wait_copies(scatter_copies(i))
+        total = sums[i][rows_at(gx * c, c), :].astype(F32)
+        for k in range(1, n):
+            total = total + lands[i][k].astype(F32)
+        fulls[i][rows_at((gy * n + gx) * c, c), :] = total.astype(BF16)
+        start_copies(gather_copies(i))
+
+    def gather_to_last(i):
+        wait_copies(gather_copies(i))
+        last_copy(i).start()
+
+    def pack(raw, value, first):
+        for j in range(-(-value.shape[1] // 128)):
+            part = value[:, j * 128 : (j + 1) * 128]
+            if part.shape[1] < 128:
+                fill_in = jnp.zeros((192, 128 - part.shape[1]), F32)
+                part = jnp.concatenate([part, fill_in], axis=1)
+            raw[(first + j) * 192 : (first + j + 1) * 192, :] = part.astype(BF16)
+
+    def unpack(out, full, first, step, width):
+        for a in range(9):
+            tile, lane = (a * step) // 128, (a * step) % 128
+            for e in range(3):
+                row = (first + tile) * 192 + e * 64
+                part = full[row : row + 64, :].astype(F32)
+                out[3 * a + e] = part[:, lane : lane + width]
+
     grad_head = jnp.zeros((64, 1), F32)
     grad_bc = jnp.zeros((64, 1), F32)
     for x in range(2):
         gs = gsr[x]
-        liquid = x0[x + 3, 2:3, 384 : 384 + 1024]
-        g = (gs * hw[...] * liquid * slope(z3[x])).astype(BF16)
+        g = (gs * hw[...] * z3[x]).astype(BF16)
         g3e[1 + x, :, inner] = g
     start_all(edge_copies(0, g3e))
     for x in range(2):
@@ -336,6 +442,8 @@
         grad_bc = grad_bc + sum_cells(g.astype(F32))
         part = wgrad(g, im2[x])
         gwc[...] = part if x == 0 else gwc[...] + part
+    pack(raw_c, gwc[...], 0)
+    pair_copy(0).start()
     finish_all(edge_copies(0, g3e))
 
     def fill_back(dst, src, x):
@@ -348,10 +456,10 @@
     for x in range(2):
         fill_back(im2.at[x], g3e, x)
         out = jnp.dot(tc[...], im2[x], preferred_element_type=F32)
-        liquid = x0[x + 3, 2:3, 384 : 384 + 1024]
-        g = merge_back(out) * liquid * slope(z2[x + 1, :, 128 : 128 + 1024])
+        g = merge_back(out) * z2[x + 1, :, 128 : 128 + 1024]
         g2e[1 + x, :, inner] = g.astype(BF16)
     start_all(edge_copies(1, g2e))
+    pair_to_scatter(0)
     for x in range(2):
         fill(im2.at[x], h1, x + 1, 128, 1024)
         g = g2e[1 + x, :, inner]
@@ -364,11 +472,14 @@
     for x in range(2):
         fill_back(im2.at[x], g2e, x)
         out = jnp.dot(tb[...], im2[x], preferred_element_type=F32)
-        liquid = x0[x + 3, 2:3, 384 : 384 + 1024]
-        g = (merge_back(out) * liquid * slope(z1[x + 2, :, 256 : 256 + 1024])).astype(BF16)
+        g = (merge_back(out) * z1[x + 2, :, 256 : 256 + 1024]).astype(BF16)
         grad_ba = grad_ba + sum_cells(g.astype(F32))
         part = wgrad(g, patches_a(x + 2, 256, 1024))
         gwa[...] = part if x == 0 else gwa[...] + part
+
+    pack(raw_b, gwb[...], 0)
+    pack(raw_b, gwa[...], 5)
+    pair_copy(1).start()
 
     lane = lax.broadcasted_iota(jnp.int32, (64, 128), 1)
     packed = jnp.where(lane == 0, grad_ba, 0.0)
@@ -376,7 +487,37 @@
     packed = jnp.where(lane == 2, grad_bc, packed)
     packed = jnp.where(lane == 3, grad_head, packed)
     packed = jnp.where(lane == 4, loss, packed)
-    small[...] = packed
+    turned = packed.T[0:8]
+    tiny[me] = jnp.concatenate([turned, turned], axis=1)
+
+    def tiny_copy(k):
+        to = lax.rem(me + k, count)
+        return pltpu.make_async_remote_copy(
+            src_ref=tiny.at[me],
+            dst_ref=tiny.at[me],
+            send_sem=ts_sem.at[k],
+            recv_sem=tr_sem.at[k],
+            device_id={"gx": to // 2, "gy": to % 2},
+            device_id_type=MESH,
+        )
+
+    tiny_copies = [tiny_copy(k) for k in range(1, count)]
+    start_copies(tiny_copies)
+    scatter_to_gather(0)
+    pair_to_scatter(1)
+    gather_to_last(0)
+    scatter_to_gather(1)
+    wait_copies(tiny_copies)
+    total = tiny[0]
+    for k in range(1, count):
+        total = total + tiny[k]
+    small[...] = total
+    wait_copies([last_copy(0)])
+    unpack(out_c, full_c, 0, 64, 64)
+    gather_to_last(1)
+    wait_copies([last_copy(1)])
+    unpack(out_b, full_b, 0, 64, 64)
+    unpack(out_a, full_b, 5, 8, 3)
 
 
 def on_device(
@@ -398,22 +539,21 @@
         w = w.reshape(3, 3, 3, 64, w.shape[-1]).transpose(2, 3, 0, 1, 4)
         return w.reshape(192, -1)
 
-    def backward(w):
-        return w.reshape(3, 3, 3, 64, 64).transpose(2, 4, 0, 1, 3).reshape(192, 576)
-
     wa = forward(jnp.pad(conv_a, ((0, 0), (0, 0), (0, 5))))
     vmem = pl.BlockSpec(memory_space=pltpu.VMEM)
     smem = pl.BlockSpec(memory_space=pltpu.SMEM)
+    chunks = tuple(-(-rows // (count * 16)) * 16 for rows in (960, 1152))
+    halves = tuple(n * c for c in chunks)
     pressure, gwa, gwb, gwc, small = pl.pallas_call(
-        functools.partial(kernel, n, float(2 * n * 16 * 128)),
+        functools.partial(kernel, n, float(2 * n * 16 * 128), chunks),
         out_shape=(
             jax.ShapeDtypeStruct((2, 8, 128), F32),
-            jax.ShapeDtypeStruct((192, 72), F32),
-            jax.ShapeDtypeStruct((192, 576), F32),
-            jax.ShapeDtypeStruct((192, 576), F32),
-            jax.ShapeDtypeStruct((64, 128), F32),
+            jax.ShapeDtypeStruct((27, 64, 3), F32),
+            jax.ShapeDtypeStruct((27, 64, 64), F32),
+            jax.ShapeDtypeStruct((27, 64, 64), F32),
+            jax.ShapeDtypeStruct((8, 128), F32),
         ),
-        in_specs=[smem] * 3 + [vmem] * 10,
+        in_specs=[smem] * 3 + [vmem] * 8,
         out_specs=(vmem,) * 5,
         scratch_shapes=[
             pltpu.VMEM((count, 64, 128), BF16),
@@ -433,32 +573,48 @@
             pltpu.VMEM((2, 1, 1024), F32),
             pltpu.VMEM((4, 64, 1280), BF16),
             pltpu.VMEM((4, 64, 1280), BF16),
+            pltpu.VMEM((192, 576), BF16),
+            pltpu.VMEM((192, 576), BF16),
+            pltpu.VMEM((192, 576), BF16),
+            pltpu.VMEM((192, 576), BF16),
+            pltpu.VMEM((192, 72), F32),
+            pltpu.VMEM((192, 576), F32),
+            pltpu.VMEM((192, 576), F32),
+            pltpu.VMEM((2 * halves[0], 128), BF16),
+            pltpu.VMEM((2 * halves[1], 128), BF16),
+            pltpu.VMEM((halves[0], 128), BF16),
+            pltpu.VMEM((halves[1], 128), BF16),
+            pltpu.VMEM((halves[0], 128), BF16),
+            pltpu.VMEM((halves[1], 128), BF16),
+            pltpu.VMEM((n, chunks[0], 128), BF16),
+            pltpu.VMEM((n, chunks[1], 128), BF16),
+            pltpu.VMEM((2 * halves[0], 128), BF16),
+            pltpu.VMEM((2 * halves[1], 128), BF16),
+            pltpu.VMEM((count, 8, 128), F32),
             pltpu.SemaphoreType.DMA((count,)),
             pltpu.SemaphoreType.DMA((count,)),
             pltpu.SemaphoreType.DMA((2, 3)),
             pltpu.SemaphoreType.DMA((2, 3)),
             pltpu.SemaphoreType.DMA((2, 5)),
             pltpu.SemaphoreType.DMA((2, 5)),
+            pltpu.SemaphoreType.DMA((2, 2 + 2 * n)),
+            pltpu.SemaphoreType.DMA((2, 2 + 2 * n)),
+            pltpu.SemaphoreType.DMA((count,)),
+            pltpu.SemaphoreType.DMA((count,)),
         ],
         compiler_params=pltpu.CompilerParams(
             collective_id=0, has_side_effects=True, vmem_limit_bytes=48 * 1024 * 1024
         ),
     )(
         brick_home, inverse_density, head_bias,
-        payload, wa, forward(conv_b), forward(conv_c), backward(conv_b), backward(conv_c),
+        payload, wa, conv_b, conv_c,
         bias_a.reshape(64, 1), bias_b.reshape(64, 1), bias_c.reshape(64, 1),
         head_weight.astype(F32).reshape(64, 1),
     )
-    gwa, gwb, gwc, small = lax.psum((gwa, gwb, gwc, small), ("gx", "gy"))
-
-    def taps(g, width):
-        g = g.reshape(3, 64, 3, 3, -1)[..., :width].transpose(2, 3, 0, 1, 4)
-        return g.reshape(27, 64, width)
-
     return (
-        pressure, small[0, 4:5],
-        taps(gwa, 3), small[:, 0], taps(gwb, 64), small[:, 1], taps(gwc, 64), small[:, 2],
-        small[:, 3],
+        pressure, small[4, 0:1],
+        gwa, small[0, 0:64], gwb, small[1, 0:64], gwc, small[2, 0:64],
+        small[3, 0:64],
     )
 
 

time: 260 us -> 74.5 us (0.29)
  waiting for transfers between devices: 186 us -> 0 us
  Pallas kernels: 41 us -> 61.4 us
  between operations: 15 us -> 1.4 us
  local copies, waits for them, and re-layouts: 17.6 us -> 9.12 us
    psum x2 -> x0, waiting for transfers between devices: 186 us -> none  [on_device(): gwa, gwb, gwc, small = lax.psum((gwa, gwb, gwc, small), ('gx', 'gy'))]
    pallas_call x1, Pallas kernels: 41 us -> 61.4 us  [on_device(): pl.pallas_call(functools.partial(kernel, n, float(2 * n * 16 * 128), chun...]
    reshape x10 -> x0, local copies, waits for them, and re-layouts: 6.54 us -> none  [the longest x4 3.3 us: forward(): w = w.reshape(3, 3, 3, 64, w.shape[-1]).transpose(2, 3, 0, 1, 4)]
    unnamed x30 -> x19, local copies, waits for them, and re-layouts: 3.77 us -> 7.43 us
    transpose x4 -> x0, local copies, waits for them, and re-layouts: 2.88 us -> none  [taps(): g = g.reshape(3, 64, 3, 3, -1)[..., :width].transpose(2, 3, 0, 1, 4)]
  transfers between devices with their start and end apart: 2 -> 0, of which waited for: 2 -> 0; matrix products, arithmetic and copies ran while one was open for 3% -> 0% of each run, Pallas kernels for 0% -> 0%
where the time goes in v1:
time: 74.5 us; the launch traced here: 74 us
  Pallas kernels  61.4 us (82%)
  local copies, waits for them, and re-layouts  9.12 us (12%)
  other arithmetic  2.07 us (3%)
  between operations  1.4 us (2%)
    pallas_call x1, Pallas kernels, on_device(): pl.pallas_call(functools.partial(kernel, n, float(2 * n * 16 * 128), chun...  61.4 us
    unnamed x19, local copies, waits for them, and re-layouts  7.43 us

profile of v1, /device:TPU:0, one launch (start us, length us, event | category | flops | bytes accessed | tf_op | source)
XLA Modules:
  0.0 74.0 jit_solution(9950209037773829132)
XLA Ops:
  1.4 0.7 bitcast_convert_fusion
  2.0 0.7 convert_bitcast_fusion
  2.7 0.7 pad_maximum_fusion.payload
  3.4 0.8 %copy.28 = bf16[27,64,3]{1,2,0:T(4,128)(2,1)S(1)} copy(bf16[27,64,3]{1,0,2:T(8,128)(2,1)} %param.18) | data formatting | bytes 20736 | tf_op args[5]
  4.2 0.1 reshape.51
  4.4 0.1 copy.30.wa
  4.5 0.0 copy-start.4
  4.5 0.1 copy.34.hw
  4.6 0.6 copy-done.4
  5.1 0.1 copy.31.ba
  5.2 0.6 copy-done.5
  5.8 0.1 copy.32.bb
  5.9 0.6 copy-done.6
  6.5 0.1 copy.33.bc
  6.6 0.6 copy-done.2
  7.1 0.0 copy-done.3
  7.1 1.0 %copy-done.1 = bf16[27,64,64]{2,1,0:T(8,128)(2,1)S(1)} copy-done((bf16[27,64,64]{2,1,0:T(8,128)(2,1)S(1)}, bf16[27,64,64]{2,1,0:T(8,128)(2,1)}, u32[]{:S(2)}) %copy-start.1) | copy-done | bytes 221208
  8.1 61.4 %shard_map.196 = (f32[2,8,128]{2,1,0:T(8,128)S(1)}, f32[27,64,3]{2,1,0:T(8,128)S(1)}, f32[27,64,64]{2,1,0:T(8,128)S(1)}, f32[27,64,64]{2,1,0:T(8,128)S(1)}, f32[8,128]{1,0:T(8,128)S(1)}) custom-call(s32[8]{0:T(128)S(1)} %copy-done.2, f32[4]{0:T(128)S(1)} %copy-done.3, f32[1]{0:T(128)S(6)} %copy.39.hbias, bf16[64,128]{1,0:T(8,128)(2,1)S(1)} %pad_maximum_fusion.payload, ...), custom_call_target="tpu_custom_call" | custom-call | tf_op jit(solution)/shard_map/pallas_call | solution.py:547
  69.6 0.5 slice.15
  70.1 0.5 slice_bitcast_fusion
  70.6 1.0 %copy.35 = f32[27,64,3]{1,0,2:T(8,128)} copy(f32[27,64,3]{2,1,0:T(8,128)S(1)} %get-tuple-element.30) | data formatting | bytes 41472
  71.6 0.6 copy.40
  72.2 0.9 %copy.41 = f32[27,64,64]{2,1,0:T(8,128)} copy(f32[27,64,64]{2,1,0:T(8,128)S(1)} %get-tuple-element.56) | data formatting | bytes 884736
  73.1 0.9 %copy.42 = f32[27,64,64]{2,1,0:T(8,128)} copy(f32[27,64,64]{2,1,0:T(8,128)S(1)} %get-tuple-element.58) | data formatting | bytes 884736
  (9 shorter events, 0.1 us)
Async XLA Ops:
  0.6 5.9 %copy-start = (bf16[27,64,64]{2,1,0:T(8,128)(2,1)S(1)}, bf16[27,64,64]{2,1,0:T(8,128)(2,1)}, u32[]{:S(2)}) copy-start(bf16[27,64,64]{2,1,0:T(8,128)(2,1)} %cb.1) | copy-start | bytes 663556
  4.5 0.7 copy-start.4
  5.1 0.7 copy-start.5
  5.8 0.7 copy-start.6
  6.5 0.7 copy-start.2
  6.5 0.7 copy-start.3
  7.1 1.0 %copy-start.1 = (bf16[27,64,64]{2,1,0:T(8,128)(2,1)S(1)}, bf16[27,64,64]{2,1,0:T(8,128)(2,1)}, u32[]{:S(2)}) copy-start(bf16[27,64,64]{2,1,0:T(8,128)(2,1)} %cc.1) | copy-start | bytes 663556
